TPU v7x, 32 devices: a whole 2x2x4 slice. The times are simulated.
32 devices in a mesh: ctx: 4 (over z), row: 2 (over y), col: 4 (over x, core).
Axes of the slice: x: 2, y: 2, z: 4, core: 2. Of those that a mesh axis runs over, the one named last changes fastest.
Arguments:
- tokens: bfloat16 [2048, 8192], P(('ctx', 'row'), 'col'), may hold values from -9 to 9
- w_query: bfloat16 [8192, 2048], P('ctx', 'col'), may hold values from -0.0625 to 0.0625
- key_value_weight: bfloat16 [8192, 512], P('ctx', 'col'), may hold values from -0.0625 to 0.0625
- segment: int32 [2048], P(('ctx', 'row')), may hold values from 0 to 7, never falling along the last dimension, each value on 1 to 1024 neighbouring positions
Outputs:
- attended: bfloat16 [2048, 2048], P(('ctx', 'row'), 'col')
Inputs may be any that keep to these rules, and one draw needn't show every extreme that they name: `segment`: document ids never fall along the sequence; a document holds 1 to 1024 tokens.
All inputs are finite; a program needn't handle non-finite values.
Results may differ from a plain program's by a relative error of at most 0.011.
Values may be sent and summed in bfloat16 or wider, within the bound.
A program may use at most 64 MiB of HBM per device.

v0:
```python
import math
import jax
import jax.numpy as jnp
from jax import lax
from jax.sharding import PartitionSpec as P


def swapped(x, axis, stride):
    return lax.ppermute(x, axis, [(i, i ^ 1 << stride) for i in range(lax.axis_size(axis))])


def passed_along(x, axis, by):
    peers = lax.axis_size(axis)
    pairs = [(i, i + by) for i in range(peers) if 0 <= i + by < peers]
    return lax.ppermute(x, axis, pairs)


def local(tokens, w_query, key_value_weight, segment):
    half = tokens.shape[0]
    head_size = key_value_weight.shape[1]
    whole = lax.all_gather(tokens, "col", axis=1, tiled=True)
    query_acc = jnp.dot(
        whole,
        lax.all_gather(w_query, "ctx", axis=0, tiled=True),
        preferred_element_type=jnp.float32,
    )
    keyval_acc = jnp.dot(
        whole,
        lax.all_gather(key_value_weight, "ctx", axis=0, tiled=True),
        preferred_element_type=jnp.float32,
    )
    query = query_acc.astype(jnp.bfloat16)
    mine = keyval_acc.astype(jnp.bfloat16)
    is_even = lax.axis_index("col") % 2 == 0
    partner = swapped(mine, "col", 0)
    joined = jnp.concatenate(
        [jnp.where(is_even, mine, partner), jnp.where(is_even, partner, mine)], axis=1
    )
    block_kv, block_seg = (
        lax.all_gather(joined, "row", axis=0, tiled=True),
        lax.all_gather(segment, "row", axis=0, tiled=True),
    )
    prev_kv, prev_seg = passed_along((block_kv, block_seg), "ctx", 1)
    heads = query.shape[1] // head_size
    queries = query.reshape(half, heads, head_size)
    block = block_kv.shape[0]
    ctx_index = lax.axis_index("ctx")
    query_pos = lax.axis_index("row") * half + jnp.arange(half)
    key_pos = jnp.arange(block)
    own_allow = (key_pos[None, :] <= query_pos[:, None]) & (segment[:, None] == block_seg[None, :])
    prev_allow = (ctx_index > 0) & (segment[:, None] == prev_seg[None, :])
    scale = 1.0 / math.sqrt(head_size)

    def scores(key_value_rows, allow):
        score = (
            jnp.einsum(
                "qhd,kd->hqk",
                queries,
                key_value_rows[:, :head_size],
                preferred_element_type=jnp.float32,
            )
            * scale
        )
        return jnp.where(allow[None], score, -jnp.inf)

    parts = [(scores(block_kv, own_allow), block_kv), (scores(prev_kv, prev_allow), prev_kv)]
    top = parts[0][0].max(axis=-1, keepdims=True)
    for score, key_value_rows in parts[1:]:
        top = jnp.maximum(top, score.max(axis=-1, keepdims=True))
    total = jnp.zeros(top.shape[:2], jnp.float32)
    numer = jnp.zeros((half, heads, head_size), jnp.float32)
    for score, key_value_rows in parts:
        weight = jnp.exp(score - top)
        total = total + jnp.sum(weight, axis=-1)
        probs = weight.astype(jnp.bfloat16)
        numer = numer + jnp.einsum(
            "hqk,kd->qhd", probs, key_value_rows[:, head_size:], preferred_element_type=jnp.float32
        )
    result = (numer / jnp.transpose(total)[:, :, None]).astype(jnp.bfloat16)
    return result.reshape(half, heads * head_size)


def solution(mesh):
    in_specs = (P(("ctx", "row"), "col"), P("ctx", "col"), P("ctx", "col"), P(("ctx", "row")))
    out_specs = P(("ctx", "row"), "col")
    return jax.shard_map(local, mesh=mesh, in_specs=in_specs, out_specs=out_specs, check_vma=False)
```

profile of v0, /device:TPU:0, one launch (start us, length us, event | category | flops | bytes accessed | tf_op | source)
XLA Modules:
  0.0 262.4 jit_solution(787395383971608503)
XLA Ops:
  6.5 0.7 all-gather.7.cloned.1.call-update
  7.3 0.0 all-gather.5.cloned.1.call-start
  7.3 0.7 all-gather.5.cloned.1.call-update
  8.0 0.0 all-gather.9.cloned.1.call-start
  8.1 0.7 all-gather.9.cloned.1.call-update
  8.8 5.2 %all-gather = s32[2,1,256]{2,1,0:T(1,128)S(1)} all-gather(s32[1,1,256]{2,1,0:T(1,128)S(1)} %bitcast.56), channel_id=1, replica_groups=mesh['ctx'=4,'row'=2,'col'=4] {'row'}, dimensions={0}, use_global_device_ids=true | all-gather | bytes 3072 | tf_op jit(solution)/shard_map/all_gather | solution.py:41
  13.9 4.0 %collective-permute-start.1 = (s32[512]{0:T(512)S(1)}, s32[512]{0:T(512)S(1)}, u32[]{:S(2)}, u32[]{:S(2)}) collective-permute-start(s32[512]{0:T(512)S(1)} %bitcast.54), channel_id=1, source_target_pairs={{0,8},{8,16},{16,24},{1,9},{9,17},{17,25},{2,10},{10,18},{18,26},{... | collective-permute-start | bytes 6152 | tf_op jit(solution)/shard_map/ppermute | solution.py:15
  18.0 39.6 %all-gather.7.cloned.1.call-done = bf16[8192,128]{1,0:T(8,128)(2,1)} async-done(((bf16[2048,128]{1,0:T(8,128)(2,1)}), bf16[8192,128]{1,0:T(8,128)(2,1)}) %all-gather.7.cloned.1.call-update) | async-done | bytes 2097168 | tf_op jit(solution)/shard_map/all_gather | solution.py:29
  57.6 34.8 %all-gather.5.cloned.1.call-done = bf16[256,8192]{1,0:T(8,128)(2,1)} async-done(((bf16[256,2048]{1,0:T(8,128)(2,1)}), bf16[256,8192]{1,0:T(8,128)(2,1)}) %all-gather.5.cloned.1.call-update) | async-done | bytes 4194320 | tf_op jit(solution)/shard_map/all_gather | solution.py:21
  92.4 4.4 %convolution_convert_fusion.1 = bf16[256,128]{0,1:T(8,128)(2,1)S(1)} fusion(bf16[256,8192]{1,0:T(8,128)(2,1)} %all-gather.5.cloned.1.call-done, bf16[8192,128]{1,0:T(8,128)(2,1)} %all-gather.7.cloned.1.call-done), kind=kOutput, calls=%fused_computation.15 | convolution fusion | flops 536903680 | bytes 6356992 | tf_op jit(solution)/shard_map/dot_general | solution.py:27
  96.8 0.3 collective-permute-start
  97.1 0.0 collective-permute-done.1
  97.1 0.3 compare_and_fusion
  97.4 0.7 collective-permute-done
  98.1 6.3 %all_gather.17 = bf16[512,256]{0,1:T(8,128)(2,1)S(1)} all-gather(bf16[256,256]{0,1:T(8,128)(2,1)S(1)} %pad_maximum_fusion), channel_id=1, replica_groups=mesh['ctx'=4,'row'=2,'col'=4] {'row'}, dimensions={0}, use_global_device_ids=true | all-gather | bytes 393216 | tf_op jit(solution)/shard_map/all_gather | solution.py:40
  104.5 3.4 %collective-permute-start.2 = (bf16[512,256]{0,1:T(8,128)(2,1)S(1)}, bf16[512,256]{0,1:T(8,128)(2,1)S(1)}, u32[]{:S(2)}, u32[]{:S(2)}) collective-permute-start(bf16[512,256]{0,1:T(8,128)(2,1)S(1)} %all_gather.17), channel_id=1, source_target_pairs={{0,8},{8,16},{16,24},{1,9},{9,17},{17,25},{2,10},{10,18},{18,26},{... | collective-permute-start | bytes 786440 | tf_op jit(solution)/shard_map/ppermute | solution.py:15
  107.9 137.2 %all-gather.9.cloned.1.call-done = bf16[8192,512]{1,0:T(8,128)(2,1)} async-done(((bf16[2048,512]{1,0:T(8,128)(2,1)}), bf16[8192,512]{1,0:T(8,128)(2,1)}) %all-gather.9.cloned.1.call-update) | async-done | bytes 8388624 | tf_op jit(solution)/shard_map/all_gather | solution.py:24
  245.1 7.0 %fusion.8 = bf16[32,4,8,128]{3,2,1,0:T(8,128)(2,1)S(1)} fusion(bf16[256,8192]{1,0:T(8,128)(2,1)} %all-gather.5.cloned.1.call-done, bf16[8192,512]{1,0:T(8,128)(2,1)} %all-gather.9.cloned.1.call-done), kind=kOutput, calls=%fused_computation.14 | convolution fusion | flops 2147614720 | bytes 12845056 | tf_op jit(solution)/shard_map/dot_general | solution.py:22
  252.1 0.5 fusion.25
  252.6 0.5 fusion.4
  253.1 0.5 fusion.10
  253.6 0.7 fusion.2
  254.3 0.7 fusion.7
  255.0 0.8 copy.18
  (9 shorter events, 0.0 us)
Async XLA Ops:
  6.5 2.2 copy-start
  6.5 51.1 %all-gather.7.cloned.1.call-start = ((), (), s32[]{:S(2)}) async-start(), calls=%async_computation.1 | async-start | bytes 2621440 | tf_op jit(solution)/shard_map/all_gather | solution.py:29
  7.3 85.1 %all-gather.5.cloned.1.call-start = ((), (), s32[]{:S(2)}) async-start(), calls=%async_computation | async-start | bytes 5242880 | tf_op jit(solution)/shard_map/all_gather | solution.py:21
  8.0 237.1 %all-gather.9.cloned.1.call-start = ((), (), s32[]{:S(2)}) async-start(), calls=%async_computation.2 | async-start | bytes 10485760 | tf_op jit(solution)/shard_map/all_gather | solution.py:24
  13.9 83.2 %collective-permute-start.1 = (s32[512]{0:T(512)S(1)}, s32[512]{0:T(512)S(1)}, u32[]{:S(2)}, u32[]{:S(2)}) collective-permute-start(s32[512]{0:T(512)S(1)} %bitcast.54), channel_id=1, source_target_pairs={{0,8},{8,16},{16,24},{1,9},{9,17},{17,25},{2,10},{10,18},{18,26},{... | collective-permute-start | bytes 6152 | tf_op jit(solution)/shard_map/ppermute | solution.py:15
  96.8 1.3 collective-permute-start
  104.5 148.1 %collective-permute-start.2 = (bf16[512,256]{0,1:T(8,128)(2,1)S(1)}, bf16[512,256]{0,1:T(8,128)(2,1)S(1)}, u32[]{:S(2)}, u32[]{:S(2)}) collective-permute-start(bf16[512,256]{0,1:T(8,128)(2,1)S(1)} %all_gather.17), channel_id=1, source_target_pairs={{0,8},{8,16},{16,24},{1,9},{9,17},{17,25},{2,10},{10,18},{18,26},{... | collective-permute-start | bytes 786440 | tf_op jit(solution)/shard_map/ppermute | solution.py:15
Sparse Core Ops, SparseCore 0:
  8.9 48.6 all-gather.6
  59.2 33.1 all-gather.4
  94.0 151.0 all-gather.8
where the time goes:
time: 263 us; the launch traced here: 262 us
  waiting for transfers between devices  214 us (81%)
  matrix products  13.6 us (5%)
  between operations  13.2 us (5%)
  blocking collectives  11.5 us (4%)
  starting transfers between devices  7.78 us (3%)
    all_gather x1, waiting for transfers between devices, local(): lax.all_gather(w_query, 'ctx', axis=0, tiled=True)  137 us
    all_gather x1, waiting for transfers between devices, local(): lax.all_gather(key_value_weight, 'ctx', axis=0, tiled=True)  39.6 us
    all_gather x1, waiting for transfers between devices, local(): whole = lax.all_gather(tokens, 'col', axis=1, tiled=True)  34.8 us
    ppermute x2, starting transfers between devices, passed_along(): return lax.ppermute(x, axis, pairs)  7.39 us
    dot_general x1, matrix products, local(): jnp.dot(whole, lax.all_gather(w_query, 'ctx', axis=0, tiled=True), prefer...  6.98 us
    all_gather x1, blocking collectives, local(): lax.all_gather(joined, 'row', axis=0, tiled=True)  6.33 us
  transfers between devices with their start and end apart: 6, of which 4 were waited for; matrix products, arithmetic and copies ran while one was open for 5% of the time, Pallas kernels for 0%

commit v1 on v0

--- a/solution.py
+++ b/solution.py
@@ -3,6 +3,28 @@
 import jax.numpy as jnp
 from jax import lax
 from jax.sharding import PartitionSpec as P
+
+
+def laid_out(blocks, dim):
+    lengths = list(blocks.shape[1:])
+    lengths[dim] *= blocks.shape[0]
+    return jnp.moveaxis(blocks, 0, dim).reshape(lengths)
+
+
+def collect(x, axis, dim):
+    devices = lax.axis_size(axis)
+    pairs = [(i, (i + 1) % devices) for i in range(devices)]
+    back = [(b, a) for a, b in pairs]
+    lower, upper = ([], [])
+    for step in range(devices - 1):
+        if step % 2 == 0:
+            lower.append(lax.ppermute(lower[-1] if lower else x, axis, pairs))
+        else:
+            upper.append(lax.ppermute(upper[-1] if upper else x, axis, back))
+    parts = jnp.stack([*lower[::-1], x, *upper])
+    shift = lax.axis_index(axis) - len(lower)
+    parts = parts[(jnp.arange(devices) - shift) % devices]
+    return laid_out(parts, dim)
 
 
 def swapped(x, axis, stride):
@@ -19,11 +41,7 @@
     half = tokens.shape[0]
     head_size = key_value_weight.shape[1]
     whole = lax.all_gather(tokens, "col", axis=1, tiled=True)
-    query_acc = jnp.dot(
-        whole,
-        lax.all_gather(w_query, "ctx", axis=0, tiled=True),
-        preferred_element_type=jnp.float32,
-    )
+    query_acc = jnp.dot(whole, collect(w_query, "ctx", 0), preferred_element_type=jnp.float32)
     keyval_acc = jnp.dot(
         whole,
         lax.all_gather(key_value_weight, "ctx", axis=0, tiled=True),

time: 263 us -> 243 us (0.924)
  waiting for transfers between devices: 214 us -> 124 us
  starting transfers between devices: 7.78 us -> 54.1 us
  local copies, waits for them, and re-layouts: 0.85 us -> 14.3 us
  other arithmetic: 1.05 us -> 12.8 us
    all_gather x1 -> x0, waiting for transfers between devices: 137 us -> none  [local(): lax.all_gather(w_query, 'ctx', axis=0, tiled=True)]
    ppermute x0 -> x3, waiting for transfers between devices: none -> 82.3 us  [the longest x2 82.3 us: collect(): lower.append(lax.ppermute(lower[-1] if lower else x, axis, pairs))]
    ppermute x2, waiting for transfers between devices: 0.01 us -> 40.4 us  [passed_along(): return lax.ppermute(x, axis, pairs)]
    all_gather x1, waiting for transfers between devices: 39.6 us -> 0.01 us  [local(): lax.all_gather(key_value_weight, 'ctx', axis=0, tiled=True)]
    all_gather x1, waiting for transfers between devices: 34.8 us -> 0.01 us  [local(): whole = lax.all_gather(tokens, 'col', axis=1, tiled=True)]
    ppermute x2, starting transfers between devices: 7.39 us -> 33.7 us  [passed_along(): return lax.ppermute(x, axis, pairs)]
    ppermute x0 -> x3, starting transfers between devices: none -> 20.3 us  [the longest x2 18.2 us: collect(): lower.append(lax.ppermute(lower[-1] if lower else x, axis, pairs))]
    gather x0 -> x3, local copies, waits for them, and re-layouts: none -> 13.4 us  [collect(): parts = parts[(jnp.arange(devices) - shift) % devices]]
  transfers between devices with their start and end apart: 6 -> 8, of which waited for: 4 -> 4; matrix products, arithmetic and copies ran while one was open for 5% -> 13% of each run, Pallas kernels for 0% -> 0%
where the time goes in v1:
time: 243 us; the launch traced here: 242 us
  waiting for transfers between devices  124 us (51%)
  starting transfers between devices  54.1 us (22%)
  local copies, waits for them, and re-layouts  14.3 us (6%)
  between operations  13.6 us (6%)
  other arithmetic  12.8 us (5%)
  matrix products  12.5 us (5%)
  blocking collectives  11 us (5%)
    ppermute x2, waiting for transfers between devices, collect(): lower.append(lax.ppermute(lower[-1] if lower else x, axis, pairs))  82.3 us
    ppermute x2, waiting for transfers between devices, passed_along(): return lax.ppermute(x, axis, pairs)  40.4 us
    ppermute x2, starting transfers between devices, passed_along(): return lax.ppermute(x, axis, pairs)  33.7 us
    ppermute x2, starting transfers between devices, collect(): lower.append(lax.ppermute(lower[-1] if lower else x, axis, pairs))  18.2 us
    gather x3, local copies, waits for them, and re-layouts, collect(): parts = parts[(jnp.arange(devices) - shift) % devices]  13.4 us
    unnamed x1, other arithmetic  7.24 us
    all_gather x1, blocking collectives, local(): lax.all_gather(joined, 'row', axis=0, tiled=True)  6.56 us
    dot_general x1, matrix products, local(): jnp.dot(whole, collect(w_query, 'ctx', 0), preferred_element_type=jnp.flo...  5.75 us
  transfers between devices with their start and end apart: 8, of which 4 were waited for; matrix products, arithmetic and copies ran while one was open for 13% of the time, Pallas kernels for 0%

profile of v1, /device:TPU:0, one launch (start us, length us, event | category | flops | bytes accessed | tf_op | source)
XLA Modules:
  0.0 242.3 jit_solution(15312077262738752954)
XLA Ops:
  6.5 0.7 all-gather.6.cloned.1.call-update
  7.3 0.7 all-gather.4.cloned.1.call-update
  8.0 3.1 %collective-permute-start.1 = (bf16[2048,512]{1,0:T(8,128)(2,1)}, bf16[2048,512]{1,0:T(8,128)(2,1)S(1)}, u32[]{:S(2)}, u32[]{:S(2)}) collective-permute-start(bf16[2048,512]{1,0:T(8,128)(2,1)} %param.5), channel_id=1, source_target_pairs={{0,8},{8,16},{16,24},{24,0},{1,9},{9,17},{17,25},{25,1},{2,10},{10... | collective-permute-start | bytes 6291464 | tf_op jit(solution)/shard_map/ppermute | solution.py:21
  11.1 2.1 collective-permute-start.3
  13.2 80.4 %collective-permute-done.1 = bf16[2048,512]{1,0:T(8,128)(2,1)S(1)} collective-permute-done((bf16[2048,512]{1,0:T(8,128)(2,1)}, bf16[2048,512]{1,0:T(8,128)(2,1)S(1)}, u32[]{:S(2)}, u32[]{:S(2)}) %collective-permute-start.1) | collective-permute-done | bytes 2097184 | tf_op jit(solution)/shard_map/ppermute | solution.py:21
  93.5 15.1 %collective-permute-start.2 = (bf16[2048,512]{1,0:T(8,128)(2,1)S(1)}, bf16[2048,512]{1,0:T(8,128)(2,1)}, u32[]{:S(2)}, u32[]{:S(2)}) collective-permute-start(bf16[2048,512]{1,0:T(8,128)(2,1)S(1)} %collective-permute-done.1), channel_id=1, source_target_pairs={{0,8},{8,16},{16,24},{24,0},{1,9},{9,17},{17,25},{25,1},{2,10},{10... | collective-permute-start | bytes 6291464 | tf_op jit(solution)/shard_map/ppermute | solution.py:21
  108.6 4.4 %all-gather = s32[2,1,256]{2,1,0:T(1,128)S(1)} all-gather(s32[1,1,256]{2,1,0:T(1,128)} %bitcast.62), channel_id=1, replica_groups=mesh['ctx'=4,'row'=2,'col'=4] {'row'}, dimensions={0}, use_global_device_ids=true | all-gather | bytes 3072 | tf_op jit(solution)/shard_map/all_gather | solution.py:59
  113.1 31.1 %collective-permute-start.4 = (s32[512]{0:T(512)S(1)}, s32[512]{0:T(512)S(1)}, u32[]{:S(2)}, u32[]{:S(2)}) collective-permute-start(s32[512]{0:T(512)S(1)} %bitcast.60), channel_id=1, source_target_pairs={{0,8},{8,16},{16,24},{1,9},{9,17},{17,25},{2,10},{10,18},{18,26},{... | collective-permute-start | bytes 6152 | tf_op jit(solution)/shard_map/ppermute | solution.py:37
  144.3 35.5 %collective-permute-done.4 = s32[512]{0:T(512)S(1)} collective-permute-done((s32[512]{0:T(512)S(1)}, s32[512]{0:T(512)S(1)}, u32[]{:S(2)}, u32[]{:S(2)}) %collective-permute-start.4) | collective-permute-done | bytes 2080 | tf_op jit(solution)/shard_map/ppermute | solution.py:37
  179.8 0.9 compare_and_fusion
  180.8 1.9 collective-permute-done.2
  182.7 3.8 %pad_maximum_fusion = bf16[4,2048,512]{2,1,0:T(8,128)(2,1)S(1)} fusion(bf16[1,2048,512]{2,1,0:T(8,128)(2,1)} %bitcast.7, bf16[1,2048,512]{2,1,0:T(8,128)(2,1)} %bitcast.55, bf16[1,2048,512]{2,1,0:T(8,128)(2,1)S(1)} %bitcast.56, bf16[1,2048,512]{2,1,0:T(8,128)(2,1)} %bitcast.4), kind=kLoop, calls=%fused_computation.2 | loop fusion | flops 12582912 | bytes 16777216 | tf_op jit(solution)/shard_map/stack | solution.py:24
  186.5 3.5 %fusion.22 = (bf16[4,1024,512]{2,1,0:T(8,128)(2,1)}, bf16[4,1024,512]{2,1,0:T(8,128)(2,1)}) fusion(bf16[4,2048,512]{2,1,0:T(8,128)(2,1)S(1)} %pad_maximum_fusion), kind=kLoop, calls=%fused_computation.47 | loop fusion | bytes 16777216 | tf_op jit(solution)/shard_map/gather | solution.py:26
  190.1 4.9 %gather_fusion.1 = bf16[4,1024,512]{2,1,0:T(8,128)(2,1)} fusion(bf16[4,1024,512]{2,1,0:T(8,128)(2,1)} %get-tuple-element.8, s32[1024]{0:T(1024)S(1)} %pad_clamp_fusion), kind=kCustom, calls=%fused_computation.1 | custom fusion | bytes 8388624 | tf_op jit(solution)/shard_map/gather | solution.py:26
  195.0 4.9 %gather_fusion = bf16[4,1024,512]{2,1,0:T(8,128)(2,1)} fusion(bf16[4,1024,512]{2,1,0:T(8,128)(2,1)} %get-tuple-element.7, s32[1024]{0:T(1024)S(1)} %pad_clamp_fusion), kind=kCustom, calls=%fused_computation | custom fusion | bytes 8388624 | tf_op jit(solution)/shard_map/gather | solution.py:26
  199.9 7.2 %pad_maximum_fusion.1 = bf16[4,2048,512]{2,1,0:T(8,128)(2,1)} fusion(bf16[4,1024,512]{2,1,0:T(8,128)(2,1)} %gather_fusion.1, bf16[4,1024,512]{2,1,0:T(8,128)(2,1)} %gather_fusion), kind=kLoop, calls=%fused_computation.3 | loop fusion | flops 16777216 | bytes 16777216
  207.2 4.5 %convolution_convert_fusion.1 = bf16[256,128]{0,1:T(8,128)(2,1)S(1)} fusion(bf16[256,8192]{1,0:T(8,128)(2,1)} %all-gather.4.cloned.1.call-done, bf16[8192,128]{1,0:T(8,128)(2,1)} %all-gather.6.cloned.1.call-done), kind=kOutput, calls=%fused_computation.18 | convolution fusion | flops 536903680 | bytes 6356992 | tf_op jit(solution)/shard_map/dot_general | solution.py:45
  211.8 5.7 %convolution_convert_fusion = bf16[512,256]{1,0:T(8,128)(2,1)S(1)} fusion(bf16[8192,512]{1,0:T(8,128)(2,1)} %bitcast.54, bf16[256,8192]{1,0:T(8,128)(2,1)S(1)} %copy-done), kind=kOutput, calls=%fused_computation.17 | convolution fusion | flops 2147614720 | bytes 12845056 | tf_op jit(solution)/shard_map/dot_general | solution.py:44
  217.6 6.6 %all_gather.14 = bf16[512,256]{0,1:T(8,128)(2,1)S(1)} all-gather(bf16[256,256]{0,1:T(8,128)(2,1)S(1)} %pad_maximum_fusion.2), channel_id=1, replica_groups=mesh['ctx'=4,'row'=2,'col'=4] {'row'}, dimensions={0}, use_global_device_ids=true | all-gather | bytes 393216 | tf_op jit(solution)/shard_map/all_gather | solution.py:58
  224.2 2.6 %collective-permute-start.5 = (bf16[512,256]{0,1:T(8,128)(2,1)S(1)}, bf16[512,256]{0,1:T(8,128)(2,1)S(1)}, u32[]{:S(2)}, u32[]{:S(2)}) collective-permute-start(bf16[512,256]{0,1:T(8,128)(2,1)S(1)} %all_gather.14), channel_id=1, source_target_pairs={{0,8},{8,16},{16,24},{1,9},{9,17},{17,25},{2,10},{10,18},{18,26},{... | collective-permute-start | bytes 786440 | tf_op jit(solution)/shard_map/ppermute | solution.py:37
  227.3 4.9 %collective-permute-done.5 = bf16[512,256]{0,1:T(8,128)(2,1)S(1)} collective-permute-done((bf16[512,256]{0,1:T(8,128)(2,1)S(1)}, bf16[512,256]{0,1:T(8,128)(2,1)S(1)}, u32[]{:S(2)}, u32[]{:S(2)}) %collective-permute-start.5) | collective-permute-done | bytes 262176 | tf_op jit(solution)/shard_map/ppermute | solution.py:37
  233.2 0.7 fusion.2
  233.9 0.7 fusion.7
  234.6 0.8 copy.18
  (19 shorter events, 1.7 us)
Async XLA Ops:
  6.5 200.7 %all-gather.6.cloned.1.call-start = ((), (), s32[]{:S(2)}) async-start(), calls=%async_computation.1 | async-start | bytes 2621440 | tf_op jit(solution)/shard_map/all_gather | solution.py:47
  7.3 199.9 %all-gather.4.cloned.1.call-start = ((), (), s32[]{:S(2)}) async-start(), calls=%async_computation | async-start | bytes 5242880 | tf_op jit(solution)/shard_map/all_gather | solution.py:43
  8.0 85.5 %collective-permute-start.1 = (bf16[2048,512]{1,0:T(8,128)(2,1)}, bf16[2048,512]{1,0:T(8,128)(2,1)S(1)}, u32[]{:S(2)}, u32[]{:S(2)}) collective-permute-start(bf16[2048,512]{1,0:T(8,128)(2,1)} %param.5), channel_id=1, source_target_pairs={{0,8},{8,16},{16,24},{24,0},{1,9},{9,17},{17,25},{25,1},{2,10},{10... | collective-permute-start | bytes 6291464 | tf_op jit(solution)/shard_map/ppermute | solution.py:21
  11.1 169.7 %collective-permute-start.3 = (bf16[2048,512]{1,0:T(8,128)(2,1)}, bf16[2048,512]{1,0:T(8,128)(2,1)}, u32[]{:S(2)}, u32[]{:S(2)}) collective-permute-start(bf16[2048,512]{1,0:T(8,128)(2,1)} %param.5), channel_id=1, source_target_pairs={{8,0},{16,8},{24,16},{0,24},{9,1},{17,9},{25,17},{1,25},{10,2},{18... | collective-permute-start | bytes 6291464 | tf_op jit(solution)/shard_map/ppermute | solution.py:23
  93.5 89.2 %collective-permute-start.2 = (bf16[2048,512]{1,0:T(8,128)(2,1)S(1)}, bf16[2048,512]{1,0:T(8,128)(2,1)}, u32[]{:S(2)}, u32[]{:S(2)}) collective-permute-start(bf16[2048,512]{1,0:T(8,128)(2,1)S(1)} %collective-permute-done.1), channel_id=1, source_target_pairs={{0,8},{8,16},{16,24},{24,0},{1,9},{9,17},{17,25},{25,1},{2,10},{10... | collective-permute-start | bytes 6291464 | tf_op jit(solution)/shard_map/ppermute | solution.py:21
  113.1 66.7 %collective-permute-start.4 = (s32[512]{0:T(512)S(1)}, s32[512]{0:T(512)S(1)}, u32[]{:S(2)}, u32[]{:S(2)}) collective-permute-start(s32[512]{0:T(512)S(1)} %bitcast.60), channel_id=1, source_target_pairs={{0,8},{8,16},{16,24},{1,9},{9,17},{17,25},{2,10},{10,18},{18,26},{... | collective-permute-start | bytes 6152 | tf_op jit(solution)/shard_map/ppermute | solution.py:37
  207.2 4.6 %copy-start = (bf16[256,8192]{1,0:T(8,128)(2,1)S(1)}, bf16[256,8192]{1,0:T(8,128)(2,1)}, u32[]{:S(2)}) copy-start(bf16[256,8192]{1,0:T(8,128)(2,1)} %all-gather.4.cloned.1.call-done) | copy-start | bytes 12582916
  211.7 5.8 %collective-permute-start = (bf16[256,128]{0,1:T(8,128)(2,1)S(1)}, bf16[256,128]{0,1:T(8,128)(2,1)S(1)}, u32[]{:S(2)}, u32[]{:S(2)}) collective-permute-start(bf16[256,128]{0,1:T(8,128)(2,1)S(1)} %convolution_convert_fusion.1), channel_id=1, source_target_pairs={{0,1},{1,0},{2,3},{3,2},{4,5},{5,4},{6,7},{7,6},{8,9},{9,8},{10,11... | collective-permute-start | bytes 196616 | tf_op jit(solution)/shard_map/ppermute | solution.py:31
  224.2 8.0 %collective-permute-start.5 = (bf16[512,256]{0,1:T(8,128)(2,1)S(1)}, bf16[512,256]{0,1:T(8,128)(2,1)S(1)}, u32[]{:S(2)}, u32[]{:S(2)}) collective-permute-start(bf16[512,256]{0,1:T(8,128)(2,1)S(1)} %all_gather.14), channel_id=1, source_target_pairs={{0,8},{8,16},{16,24},{1,9},{9,17},{17,25},{2,10},{10,18},{18,26},{... | collective-permute-start | bytes 786440 | tf_op jit(solution)/shard_map/ppermute | solution.py:37
Sparse Core Ops, SparseCore 0:
  8.9 101.0 all-gather.5
  111.6 32.6 all-gather.3
